TPU v7x, 256 devices: a whole 4x4x8 slice. The times are simulated.
256 devices in a mesh: dp: 32 (over z_lo, y, core), feat: 8 (over z_hi, x).
Axes of the slice: x: 4, y: 4, z: 8 (z_hi: 2, z_lo: 4; z = z_hi * 4 + z_lo), core: 2. Of those that a mesh axis runs over, the one named last changes fastest.
Arguments:
- table: bfloat16 [4096, 3584], P('dp', 'feat'), may hold values from -64 to 64
- text: bfloat16 [4096, 3584], P('dp', 'feat'), may hold values from -64 to 64
- table_proj: bfloat16 [3584, 4096], P(None, 'feat'), may hold values from -1 to 1
- text_proj: bfloat16 [3584, 4096], P(None, 'feat'), may hold values from -1 to 1
Outputs:
- grad_table: float32 [4096, 3584], P('dp', 'feat')
- grad_text: float32 [4096, 3584], P('dp', 'feat')
- loss_mean: float32 [1], replicated
All inputs are finite; a program needn't handle non-finite values.
Results may differ from a plain program's by a relative error of at most 0.0044.
Values may be sent and summed in bfloat16 or wider, within the bound.
A program may use at most 64 MiB of HBM per device.

v0:
```python
import jax
import jax.numpy as jnp
from jax import lax
from jax.sharding import PartitionSpec as P

OFF_WEIGHT = 0.1
EPS = 1e-05


def normalize(proj, total, squares, pairs):
    center = total / pairs
    spread = squares / pairs - center * center
    inverse = lax.rsqrt(spread + EPS)
    return ((proj - center) * inverse, inverse)


def kernel_block(corr_block, row_index, col_index):
    on_diag = row_index[:, None] == col_index[None, :]
    terms = jnp.where(
        on_diag, (1.0 - corr_block) * (1.0 - corr_block), OFF_WEIGHT * corr_block * corr_block
    )
    kernel = jnp.where(on_diag, corr_block - 1.0, OFF_WEIGHT * corr_block).astype(jnp.bfloat16)
    return (kernel, jnp.sum(terms))


def body(table, text, table_proj, text_proj):
    full_table, full_text = (
        lax.all_gather(table, "feat", axis=1, tiled=True),
        lax.all_gather(text, "feat", axis=1, tiled=True),
    )
    z_table = jnp.dot(full_table, table_proj, preferred_element_type=jnp.float32)
    z_text = jnp.dot(full_text, text_proj, preferred_element_type=jnp.float32)
    sum_table, sq_table, sum_text, sq_text = lax.psum(
        (
            jnp.sum(z_table, axis=0),
            jnp.sum(z_table * z_table, axis=0),
            jnp.sum(z_text, axis=0),
            jnp.sum(z_text * z_text, axis=0),
        ),
        "dp",
    )
    num_dp = lax.axis_size("dp")
    local_rows = z_table.shape[0]
    pairs = local_rows * num_dp
    normed_table, inverse_table = normalize(z_table, sum_table, sq_table, pairs)
    normed_text, inverse_text = normalize(z_text, sum_text, sq_text, pairs)
    half_table = normed_table.astype(jnp.bfloat16)
    half_text = normed_text.astype(jnp.bfloat16)
    text_full = lax.all_gather(half_text, "feat", axis=1, tiled=True)
    local_feats = half_table.shape[1]
    all_feats = text_full.shape[1]
    dp_index = lax.axis_index("dp")
    feat_index = lax.axis_index("feat")
    sub_width = all_feats // num_dp
    text_sub = lax.all_to_all(text_full, "dp", split_axis=1, concat_axis=0, tiled=True)
    corr_block = (
        lax.dot_general(
            lax.all_gather(half_table, "dp", axis=0, tiled=True),
            text_sub,
            (((0,), (0,)), ((), ())),
            preferred_element_type=jnp.float32,
        )
        / pairs
    )
    row_index = feat_index * local_feats + jnp.arange(local_feats, dtype=jnp.int32)
    col_index = dp_index * sub_width + jnp.arange(sub_width, dtype=jnp.int32)
    kernel, loss_part = kernel_block(corr_block, row_index, col_index)
    kernel_local = lax.all_gather(kernel, "dp", axis=1, tiled=True)
    loss_total = lax.psum(loss_part, ("dp", "feat"))
    loss_mean = (loss_total / all_feats).reshape(1)
    d_table = lax.dot_general(
        text_full, kernel_local, (((1,), (1,)), ((), ())), preferred_element_type=jnp.float32
    )
    text_terms = jnp.dot(half_table, kernel_local, preferred_element_type=jnp.float32)
    d_text = lax.psum_scatter(text_terms, "feat", scatter_dimension=1, tiled=True)
    mean_table, tilt_table, mean_text, tilt_text = lax.psum(
        (
            jnp.sum(d_table, axis=0),
            jnp.sum(d_table * normed_table, axis=0),
            jnp.sum(d_text, axis=0),
            jnp.sum(d_text * normed_text, axis=0),
        ),
        "dp",
    )
    back_table = (
        inverse_table * (d_table - mean_table / pairs - normed_table * (tilt_table / pairs))
    ).astype(jnp.bfloat16)
    back_text = (
        inverse_text * (d_text - mean_text / pairs - normed_text * (tilt_text / pairs))
    ).astype(jnp.bfloat16)
    table_terms = lax.dot_general(
        back_table, table_proj, (((1,), (1,)), ((), ())), preferred_element_type=jnp.float32
    )
    text_embed_terms = lax.dot_general(
        back_text, text_proj, (((1,), (1,)), ((), ())), preferred_element_type=jnp.float32
    )
    grad_table, grad_text = (
        lax.psum_scatter(table_terms, "feat", scatter_dimension=1, tiled=True),
        lax.psum_scatter(text_embed_terms, "feat", scatter_dimension=1, tiled=True),
    )
    return (grad_table, grad_text, loss_mean)


def solution(mesh):
    placed = (P("dp", "feat"), P("dp", "feat"), P(None, "feat"), P(None, "feat"))
    return jax.shard_map(
        body,
        mesh=mesh,
        in_specs=placed,
        out_specs=(P("dp", "feat"), P("dp", "feat"), P()),
        check_vma=False,
    )
```

profile of v0, /device:TPU:8, one launch (start us, length us, event | category | flops | bytes accessed | tf_op | source)
XLA Modules:
  0.0 741.1 jit_solution(3149157199122691087)
XLA Ops:
  7.2 0.0 all-gather.4.cloned.1.call-start
  7.2 48.1 %all_gather.15 = bf16[128,3584]{0,1:T(8,128)(2,1)S(1)} all-gather(bf16[128,448]{0,1:T(8,128)(2,1)} %param.4), channel_id=1, replica_groups=mesh['dp'=32,'feat'=8] {'feat'}, dimensions={1}, use_global_device_ids=true | all-gather | bytes 1032192 | tf_op jit(solution)/shard_map/all_gather | solution.py:28
  55.3 46.5 %all_gather.16 = bf16[128,3584]{0,1:T(8,128)(2,1)S(1)} all-gather(bf16[128,448]{0,1:T(8,128)(2,1)} %param.5), channel_id=1, replica_groups=mesh['dp'=32,'feat'=8] {'feat'}, dimensions={1}, use_global_device_ids=true | all-gather | bytes 1032192 | tf_op jit(solution)/shard_map/all_gather | solution.py:29
  101.9 2.7 multiply_reduce_fusion.3
  104.6 0.7 fusion.16
  105.3 62.6 %all-reduce.1 = (f32[512]{0:T(512)S(1)}, f32[512]{0:T(512)S(1)}, f32[512]{0:T(512)S(1)}, f32[512]{0:T(512)S(1)}) all-reduce(f32[512]{0:T(512)S(1)} %get-tuple-element.10, f32[512]{0:T(512)S(1)} %get-tuple-element.9, f32[512]{0:T(512)S(1)} %get-tuple-element.8, f32[512]{0:T(512)S(1)} %get-tuple-element.7), channel_id=1, replica_groups=mesh['dp'=32,'feat'=8] {'dp'}, use_global_device_ids=true, to_apply=%region_7.0 | all-reduce | flops 2048 | bytes 16384 | tf_op jit(solution)/shard_map/psum | solution.py:33
  167.9 0.7 fusion.2
  168.6 0.0 all-gather.4.cloned.1.call-update
  168.6 0.0 all-gather.6.cloned.1.call-start
  168.7 0.7 fusion.3
  169.4 65.7 %all-gather.4.cloned.1.call-done = bf16[128,4096]{1,0:T(8,128)(2,1)} async-done(((bf16[128,512]{1,0:T(8,128)(2,1)}), bf16[128,4096]{1,0:T(8,128)(2,1)}) %all-gather.4.cloned.1.call-update) | async-done | bytes 1048592 | tf_op jit(solution)/shard_map/all_gather | solution.py:49
  235.1 2.5 copy_bitcast_fusion
  237.6 5.1 all-to-all-start
  242.7 0.0 all-gather.8.cloned.1.call-start
  242.8 34.9 %all-to-all-done = bf16[128,32,128]{2,0,1:T(8,128)(2,1)S(1)} async-done(((bf16[128,32,128]{2,0,1:T(8,128)(2,1)}), bf16[128,32,128]{2,0,1:T(8,128)(2,1)S(1)}, u32[]{:S(2)}, u32[]{:S(2)}) %all-to-all-start) | async-done | bytes 1048608 | tf_op jit(solution)/shard_map/all_to_all | solution.py:55
  277.7 27.7 %all-gather.6.cloned.1.call-done = bf16[4096,512]{1,0:T(8,128)(2,1)} async-done(((bf16[128,512]{1,0:T(8,128)(2,1)}), bf16[4096,512]{1,0:T(8,128)(2,1)}) %all-gather.6.cloned.1.call-update) | async-done | bytes 4194320 | tf_op jit(solution)/shard_map/all_gather | solution.py:58
  305.4 4.7 fusion.1
  310.2 0.0 all-gather.8.cloned.1.call-update
  310.2 0.0 reduce-scatter.6.cloned.1.call-start
  310.2 69.1 %all-gather.8.cloned.1.call-done = bf16[512,4096]{1,0:T(8,128)(2,1)} async-done(((bf16[512,128]{1,0:T(8,128)(2,1)}), bf16[512,4096]{1,0:T(8,128)(2,1)}) %all-gather.8.cloned.1.call-update) | async-done | bytes 4194320 | tf_op jit(solution)/shard_map/all_gather | solution.py:68
  379.3 4.2 fusion.17
  383.6 0.0 reduce-scatter.8.cloned.1.call-start
  383.7 3.7 fusion.15
  387.4 91.5 %reduce-scatter.6.cloned.1.call-done = f32[128,512]{1,0:T(8,128)} async-done(((f32[128,4096]{1,0:T(8,128)}), f32[128,512]{1,0:T(8,128)}) %reduce-scatter.6.cloned.1.call-update) | async-done | bytes 262160 | tf_op jit(solution)/shard_map/reduce_scatter | solution.py:75
  478.9 1.0 fusion.14
  479.9 63.0 %all-reduce = (f32[512]{0:T(512)S(1)}, f32[512]{0:T(512)S(1)}, f32[512]{0:T(512)S(1)}, f32[512]{0:T(512)S(1)}) all-reduce(f32[512]{0:T(512)S(1)} %get-tuple-element.6, f32[512]{0:T(512)S(1)} %get-tuple-element.5, f32[512]{0:T(512)S(1)} %get-tuple-element.4, f32[512]{0:T(512)S(1)} %get-tuple-element.3), channel_id=1, replica_groups=mesh['dp'=32,'feat'=8] {'dp'}, use_global_device_ids=true, to_apply=%region_11.12 | all-reduce | flops 2048 | bytes 16384 | tf_op jit(solution)/shard_map/psum | solution.py:76
  542.9 4.5 fusion.5
  547.5 0.0 reduce-scatter.4.cloned.1.call-start
  547.5 4.4 fusion.4
  552.0 81.6 %psum.71 = f32[]{:T(128)} all-reduce(f32[]{:T(128)} %get-tuple-element.19), channel_id=1, replica_groups=mesh['dp'=32,'feat'=8] {'dp','feat'}, use_global_device_ids=true, to_apply=%region_20.21 | all-reduce | flops 1 | bytes 8 | tf_op jit(solution)/shard_map/psum | solution.py:69
  634.3 5.3 reduce-scatter.8.cloned.1.call-done
  639.6 93.6 %reduce-scatter.4.cloned.1.call-done = f32[128,448]{0,1:T(8,128)} async-done(((f32[128,3584]{0,1:T(8,128)}), f32[128,448]{0,1:T(8,128)}) %reduce-scatter.4.cloned.1.call-update) | async-done | bytes 229392 | tf_op jit(solution)/shard_map/reduce_scatter | solution.py:98
  (16 shorter events, 0.1 us)
Async XLA Ops:
  7.2 227.9 %all-gather.4.cloned.1.call-start = ((), (), s32[]{:S(2)}) async-start(), calls=%async_computation.4 | async-start | bytes 1179648 | tf_op jit(solution)/shard_map/all_gather | solution.py:49
  7.2 97.4 %copy-start = (bf16[3584,512]{1,0:T(8,128)(2,1)S(1)}, bf16[3584,512]{1,0:T(8,128)(2,1)}, u32[]{:S(2)}) copy-start(bf16[3584,512]{1,0:T(8,128)(2,1)} %param.7) | copy-start | bytes 11010052
  168.6 136.8 %all-gather.6.cloned.1.call-start = ((), (), s32[]{:S(2)}) async-start(), calls=%async_computation.5 | async-start | bytes 4325376 | tf_op jit(solution)/shard_map/all_gather | solution.py:58
  237.6 40.1 %all-to-all-start = ((bf16[128,32,128]{2,0,1:T(8,128)(2,1)}), bf16[128,32,128]{2,0,1:T(8,128)(2,1)S(1)}, u32[]{:S(2)}, u32[]{:S(2)}) async-start(bf16[128,32,128]{2,0,1:T(8,128)(2,1)} %copy_bitcast_fusion), calls=%async_computation | async-start | bytes 2097152 | tf_op jit(solution)/shard_map/all_to_all | solution.py:55
  242.7 136.6 %copy-start.2 = (bf16[128,512]{1,0:T(8,128)(2,1)S(1)}, bf16[128,512]{1,0:T(8,128)(2,1)}, u32[]{:S(2)}) copy-start(bf16[128,512]{1,0:T(8,128)(2,1)} %fusion.3) | copy-start | bytes 393220
  242.7 136.6 %all-gather.8.cloned.1.call-start = ((), (), s32[]{:S(2)}) async-start(), calls=%async_computation.6 | async-start | bytes 4325376 | tf_op jit(solution)/shard_map/all_gather | solution.py:68
  310.2 73.5 %copy-start.1 = (bf16[128,4096]{1,0:T(8,128)(2,1)S(1)}, bf16[128,4096]{1,0:T(8,128)(2,1)}, u32[]{:S(2)}) copy-start(bf16[128,4096]{1,0:T(8,128)(2,1)} %all-gather.4.cloned.1.call-done) | copy-start | bytes 3145732
  310.2 168.7 %reduce-scatter.6.cloned.1.call-start = ((), (), s32[]{:S(2)}) async-start(), calls=%async_computation.8 | async-start | bytes 2359296 | tf_op jit(solution)/shard_map/reduce_scatter | solution.py:75
  383.6 256.0 %reduce-scatter.8.cloned.1.call-start = ((), (), s32[]{:S(2)}) async-start(), calls=%async_computation.9 | async-start | bytes 2064384 | tf_op jit(solution)/shard_map/reduce_scatter | solution.py:99
  547.5 185.7 %reduce-scatter.4.cloned.1.call-start = ((), (), s32[]{:S(2)}) async-start(), calls=%async_computation.7 | async-start | bytes 2064384 | tf_op jit(solution)/shard_map/reduce_scatter | solution.py:98
Sparse Core Ops, SparseCore 0:
  168.8 66.2 all-gather.3
  237.5 67.8 all-gather.5
  310.3 68.9 all-gather.7
  383.7 95.0 reduce-scatter.5
  547.6 91.9 reduce-scatter.7
  644.6 88.4 reduce-scatter.3
where the time goes:
time: 742 us; the launch traced here: 741 us
  waiting for transfers between devices  388 us (52%)
  blocking collectives  302 us (41%)
  matrix products  25.1 us (3%)
  between operations  16 us (2%)
    reduce_scatter x1, waiting for transfers between devices, body(): lax.psum_scatter(table_terms, 'feat', scatter_dimension=1, tiled=True)  93.6 us
    reduce_scatter x1, waiting for transfers between devices, body(): lax.psum_scatter(text_terms, 'feat', scatter_dimension=1, tiled=True)  91.5 us
    psum x1, blocking collectives, body(): loss_total = lax.psum(loss_part, ('dp', 'feat'))  81.6 us
    all_gather x1, waiting for transfers between devices, body(): kernel_local = lax.all_gather(kernel, 'dp', axis=1, tiled=True)  69.1 us
    all_gather x1, waiting for transfers between devices, body(): text_full = lax.all_gather(half_text, 'feat', axis=1, tiled=True)  65.7 us
    psum x1, blocking collectives, body(): lax.psum((jnp.sum(d_table, axis=0), jnp.sum(d_table * normed_table, axis=...  63 us
    psum x1, blocking collectives, body(): lax.psum((jnp.sum(z_table, axis=0), jnp.sum(z_table * z_table, axis=0), j...  62.6 us
    all_gather x1, blocking collectives, body(): lax.all_gather(table, 'feat', axis=1, tiled=True)  48.1 us
  transfers between devices with their start and end apart: 7, of which 7 were waited for; matrix products, arithmetic and copies ran while one was open for 2% of the time, Pallas kernels for 0%

commit v1 on v0

--- a/solution.py
+++ b/solution.py
@@ -25,7 +25,9 @@
 
 def body(table, text, table_proj, text_proj):
     full_table, full_text = (
-        lax.all_gather(table, "feat", axis=1, tiled=True),
+        jnp.concatenate(
+            lax.all_to_all(jnp.stack([table] * lax.axis_size("feat")), "feat", 0, 0), axis=1
+        ),
         lax.all_gather(text, "feat", axis=1, tiled=True),
     )
     z_table = jnp.dot(full_table, table_proj, preferred_element_type=jnp.float32)

time: 742 us -> 720 us (0.970)
  blocking collectives: 302 us -> 269 us
  starting transfers between devices: 5.35 us -> 16.3 us
    all_gather x1 -> x0, blocking collectives: 48.1 us -> none  [body(): lax.all_gather(table, 'feat', axis=1, tiled=True)]
    all_gather x1, blocking collectives: 46.5 us -> 61.5 us  [body(): lax.all_gather(text, 'feat', axis=1, tiled=True)]
    all_to_all x0 -> x1, starting transfers between devices: none -> 10.9 us  [body(): lax.all_to_all(jnp.stack([table] * lax.axis_size('feat')), 'feat', 0, 0)]
  transfers between devices with their start and end apart: 7 -> 8, of which waited for: 7 -> 7; matrix products, arithmetic and copies ran while one was open for 2% -> 2% of each run, Pallas kernels for 0% -> 0%
where the time goes in v1:
time: 720 us; the launch traced here: 719 us
  waiting for transfers between devices  384 us (53%)
  blocking collectives  269 us (37%)
  matrix products  27.1 us (4%)
  starting transfers between devices  16.3 us (2%)
  between operations  16 us (2%)
    reduce_scatter x1, waiting for transfers between devices, body(): lax.psum_scatter(table_terms, 'feat', scatter_dimension=1, tiled=True)  93.6 us
    reduce_scatter x1, waiting for transfers between devices, body(): lax.psum_scatter(text_terms, 'feat', scatter_dimension=1, tiled=True)  91.7 us
    psum x1, blocking collectives, body(): loss_total = lax.psum(loss_part, ('dp', 'feat'))  81.1 us
    all_gather x1, waiting for transfers between devices, body(): kernel_local = lax.all_gather(kernel, 'dp', axis=1, tiled=True)  69.1 us
    psum x1, blocking collectives, body(): lax.psum((jnp.sum(d_table, axis=0), jnp.sum(d_table * normed_table, axis=...  63 us
    psum x1, blocking collectives, body(): lax.psum((jnp.sum(z_table, axis=0), jnp.sum(z_table * z_table, axis=0), j...  63 us
    all_gather x1, blocking collectives, body(): lax.all_gather(text, 'feat', axis=1, tiled=True)  61.5 us
    all_gather x1, waiting for transfers between devices, body(): text_full = lax.all_gather(half_text, 'feat', axis=1, tiled=True)  60.9 us
  transfers between devices with their start and end apart: 8, of which 7 were waited for; matrix products, arithmetic and copies ran while one was open for 2% of the time, Pallas kernels for 0%

profile of v1, /device:TPU:8, one launch (start us, length us, event | category | flops | bytes accessed | tf_op | source)
XLA Modules:
  0.0 719.1 jit_solution(6438359261555881822)
XLA Ops:
  7.2 1.9 stack.2
  9.1 10.9 %all-to-all-start = ((bf16[8,128,448]{1,2,0:T(8,128)(2,1)}), bf16[8,128,448]{1,2,0:T(8,128)(2,1)S(1)}, u32[]{:S(2)}, u32[]{:S(2)}) async-start(bf16[8,128,448]{1,2,0:T(8,128)(2,1)} %stack.2), calls=%async_computation | async-start | bytes 1835008 | tf_op jit(solution)/shard_map/all_to_all | solution.py:29
  20.0 0.0 all-gather.4.cloned.1.call-start
  20.1 61.5 %all_gather.12 = bf16[128,3584]{0,1:T(8,128)(2,1)S(1)} all-gather(bf16[128,448]{0,1:T(8,128)(2,1)} %param.5), channel_id=1, replica_groups=mesh['dp'=32,'feat'=8] {'feat'}, dimensions={1}, use_global_device_ids=true | all-gather | bytes 1032192 | tf_op jit(solution)/shard_map/all_gather | solution.py:31
  81.6 2.7 fusion.16
  84.4 2.7 multiply_reduce_fusion.3
  87.1 63.0 %all-reduce.1 = (f32[512]{0:T(512)S(1)}, f32[512]{0:T(512)S(1)}, f32[512]{0:T(512)S(1)}, f32[512]{0:T(512)S(1)}) all-reduce(f32[512]{0:T(512)S(1)} %get-tuple-element.10, f32[512]{0:T(512)S(1)} %get-tuple-element.9, f32[512]{0:T(512)S(1)} %get-tuple-element.8, f32[512]{0:T(512)S(1)} %get-tuple-element.7), channel_id=1, replica_groups=mesh['dp'=32,'feat'=8] {'dp'}, use_global_device_ids=true, to_apply=%region_7.0 | all-reduce | flops 2048 | bytes 16384 | tf_op jit(solution)/shard_map/psum | solution.py:35
  150.1 0.7 fusion.2
  150.8 0.0 all-gather.6.cloned.1.call-start
  150.9 0.7 fusion.3
  151.5 0.0 all-gather.6.cloned.1.call-update
  151.6 60.9 %all-gather.4.cloned.1.call-done = bf16[128,4096]{1,0:T(8,128)(2,1)} async-done(((bf16[128,512]{1,0:T(8,128)(2,1)}), bf16[128,4096]{1,0:T(8,128)(2,1)}) %all-gather.4.cloned.1.call-update) | async-done | bytes 1048592 | tf_op jit(solution)/shard_map/all_gather | solution.py:51
  212.5 2.5 copy_bitcast_fusion
  215.0 5.1 all-to-all-start.1
  220.1 0.0 all-gather.8.cloned.1.call-start
  220.2 34.9 %all-to-all-done.1 = bf16[128,32,128]{2,0,1:T(8,128)(2,1)S(1)} async-done(((bf16[128,32,128]{2,0,1:T(8,128)(2,1)}), bf16[128,32,128]{2,0,1:T(8,128)(2,1)S(1)}, u32[]{:S(2)}, u32[]{:S(2)}) %all-to-all-start.1) | async-done | bytes 1048608 | tf_op jit(solution)/shard_map/all_to_all | solution.py:57
  255.1 27.7 %all-gather.6.cloned.1.call-done = bf16[4096,512]{1,0:T(8,128)(2,1)} async-done(((bf16[128,512]{1,0:T(8,128)(2,1)}), bf16[4096,512]{1,0:T(8,128)(2,1)}) %all-gather.6.cloned.1.call-update) | async-done | bytes 4194320 | tf_op jit(solution)/shard_map/all_gather | solution.py:60
  282.8 4.7 fusion.1
  287.6 0.0 reduce-scatter.6.cloned.1.call-start
  287.6 69.1 %all-gather.8.cloned.1.call-done = bf16[512,4096]{1,0:T(8,128)(2,1)} async-done(((bf16[512,128]{1,0:T(8,128)(2,1)}), bf16[512,4096]{1,0:T(8,128)(2,1)}) %all-gather.8.cloned.1.call-update) | async-done | bytes 4194320 | tf_op jit(solution)/shard_map/all_gather | solution.py:70
  356.7 4.2 fusion.17
  361.0 0.0 reduce-scatter.8.cloned.1.call-start
  361.1 3.7 fusion.15
  364.8 91.7 %reduce-scatter.6.cloned.1.call-done = f32[128,512]{1,0:T(8,128)} async-done(((f32[128,4096]{1,0:T(8,128)}), f32[128,512]{1,0:T(8,128)}) %reduce-scatter.6.cloned.1.call-update) | async-done | bytes 262160 | tf_op jit(solution)/shard_map/reduce_scatter | solution.py:77
  456.5 1.0 fusion.14
  457.5 63.0 %all-reduce = (f32[512]{0:T(512)S(1)}, f32[512]{0:T(512)S(1)}, f32[512]{0:T(512)S(1)}, f32[512]{0:T(512)S(1)}) all-reduce(f32[512]{0:T(512)S(1)} %get-tuple-element.6, f32[512]{0:T(512)S(1)} %get-tuple-element.5, f32[512]{0:T(512)S(1)} %get-tuple-element.4, f32[512]{0:T(512)S(1)} %get-tuple-element.3), channel_id=1, replica_groups=mesh['dp'=32,'feat'=8] {'dp'}, use_global_device_ids=true, to_apply=%region_11.12 | all-reduce | flops 2048 | bytes 16384 | tf_op jit(solution)/shard_map/psum | solution.py:78
  520.6 4.5 fusion.5
  525.1 0.0 reduce-scatter.4.cloned.1.call-start
  525.2 4.4 fusion.4
  529.6 81.1 %psum.71 = f32[]{:T(128)} all-reduce(f32[]{:T(128)} %get-tuple-element.19), channel_id=1, replica_groups=mesh['dp'=32,'feat'=8] {'dp','feat'}, use_global_device_ids=true, to_apply=%region_20.21 | all-reduce | flops 1 | bytes 8 | tf_op jit(solution)/shard_map/psum | solution.py:71
  611.4 6.2 reduce-scatter.8.cloned.1.call-done
  617.6 93.6 %reduce-scatter.4.cloned.1.call-done = f32[128,448]{0,1:T(8,128)} async-done(((f32[128,3584]{0,1:T(8,128)}), f32[128,448]{0,1:T(8,128)}) %reduce-scatter.4.cloned.1.call-update) | async-done | bytes 229392 | tf_op jit(solution)/shard_map/reduce_scatter | solution.py:100
  (16 shorter events, 0.1 us)
Async XLA Ops:
  9.1 75.2 %all-to-all-start = ((bf16[8,128,448]{1,2,0:T(8,128)(2,1)}), bf16[8,128,448]{1,2,0:T(8,128)(2,1)S(1)}, u32[]{:S(2)}, u32[]{:S(2)}) async-start(bf16[8,128,448]{1,2,0:T(8,128)(2,1)} %stack.2), calls=%async_computation | async-start | bytes 1835008 | tf_op jit(solution)/shard_map/all_to_all | solution.py:29
  20.0 192.5 %all-gather.4.cloned.1.call-start = ((), (), s32[]{:S(2)}) async-start(), calls=%async_computation.5 | async-start | bytes 1179648 | tf_op jit(solution)/shard_map/all_gather | solution.py:51
  150.8 132.0 %all-gather.6.cloned.1.call-start = ((), (), s32[]{:S(2)}) async-start(), calls=%async_computation.6 | async-start | bytes 4325376 | tf_op jit(solution)/shard_map/all_gather | solution.py:60
  215.0 40.1 %all-to-all-start.1 = ((bf16[128,32,128]{2,0,1:T(8,128)(2,1)}), bf16[128,32,128]{2,0,1:T(8,128)(2,1)S(1)}, u32[]{:S(2)}, u32[]{:S(2)}) async-start(bf16[128,32,128]{2,0,1:T(8,128)(2,1)} %copy_bitcast_fusion), calls=%async_computation.1 | async-start | bytes 2097152 | tf_op jit(solution)/shard_map/all_to_all | solution.py:57
  220.1 136.6 %copy-start.1 = (bf16[128,512]{1,0:T(8,128)(2,1)S(1)}, bf16[128,512]{1,0:T(8,128)(2,1)}, u32[]{:S(2)}) copy-start(bf16[128,512]{1,0:T(8,128)(2,1)} %fusion.3) | copy-start | bytes 393220
  220.1 136.6 %all-gather.8.cloned.1.call-start = ((), (), s32[]{:S(2)}) async-start(), calls=%async_computation.7 | async-start | bytes 4325376 | tf_op jit(solution)/shard_map/all_gather | solution.py:70
  287.6 73.5 %copy-start = (bf16[128,4096]{1,0:T(8,128)(2,1)S(1)}, bf16[128,4096]{1,0:T(8,128)(2,1)}, u32[]{:S(2)}) copy-start(bf16[128,4096]{1,0:T(8,128)(2,1)} %all-gather.4.cloned.1.call-done) | copy-start | bytes 3145732
  287.6 168.9 %reduce-scatter.6.cloned.1.call-start = ((), (), s32[]{:S(2)}) async-start(), calls=%async_computation.9 | async-start | bytes 2359296 | tf_op jit(solution)/shard_map/reduce_scatter | solution.py:77
  361.0 256.6 %reduce-scatter.8.cloned.1.call-start = ((), (), s32[]{:S(2)}) async-start(), calls=%async_computation.10 | async-start | bytes 2064384 | tf_op jit(solution)/shard_map/reduce_scatter | solution.py:101
  525.1 186.0 %reduce-scatter.4.cloned.1.call-start = ((), (), s32[]{:S(2)}) async-start(), calls=%async_computation.8 | async-start | bytes 2064384 | tf_op jit(solution)/shard_map/reduce_scatter | solution.py:100
Sparse Core Ops, SparseCore 0:
  150.9 61.5 all-gather.3
  214.9 67.8 all-gather.5
  287.7 69.0 all-gather.7
  361.1 95.3 reduce-scatter.5
  525.3 92.3 reduce-scatter.7
  622.7 88.4 reduce-scatter.3
